TPU v7x, 32 devices: a whole 2x2x4 slice. The times are simulated.
32 devices in a mesh: gx: 8 (over z, x), gy: 2 (over y), gz: 2 (over core).
Axes of the slice: x: 2, y: 2, z: 4, core: 2. Of those that a mesh axis runs over, the one named last changes fastest.
Arguments:
- tokens: bfloat16 [2, 16, 4, 18432], P('gz', 'gy', None, 'gx'), may hold values from -40 to 40
- norm_gain: float32 [18432], P('gx'), may hold values from 0.2 to 1.8
- w_query: bfloat16 [18432, 12288], P('gx', 'gy'), may hold values from -0.046875 to 0.046875
- w_keyval: bfloat16 [18432, 512], P('gx', 'gy'), may hold values from -0.109375 to 0.109375
- cache_keys: bfloat16 [2, 16, 8192, 256], P('gz', ('gx', 'gy')), may hold values from -800 to 800
- cache_values: bfloat16 [2, 16, 8192, 256], P('gz', ('gx', 'gy')), may hold values from -6 to 6
- lengths: int32 [2, 16], P('gz', ('gx', 'gy')), may hold values from 1024 to 8192, as said below
Outputs:
- attended: bfloat16 [2, 16, 4, 12288], P('gz', ('gx', 'gy'))
- new_entries: bfloat16 [2, 16, 4, 512], P('gz', ('gx', 'gy'))
Inputs may be any that keep to these rules, and one draw needn't show every extreme that they name: `lengths`: some sequence uses all 8192 positions.
All inputs are finite; a program needn't handle non-finite values.
Results may differ from a plain program's by a relative error of at most 0.02.
Values may be sent and summed in bfloat16 or wider, within the bound.
A program may use at most 64 MiB of HBM per device.

v0:
```python
import jax
import jax.numpy as jnp
from jax import lax
from jax.sharding import PartitionSpec as P

D = 18432


def normalize(row_block, gain_part):
    values = row_block.astype(jnp.float32)
    row_sum, row_square = lax.psum(
        (jnp.sum(values, axis=-1), jnp.sum(values * values, axis=-1)), "gx"
    )
    center = row_sum / D
    spread = row_square / D - center * center
    factor = lax.rsqrt(spread + 1e-05)
    return ((values - center[..., None]) * factor[..., None] * gain_part).astype(jnp.bfloat16)


def project(normed, w_query, w_keyval):
    gathered = lax.all_gather(normed, "gy", axis=0, tiled=True)
    row_total, step_total, local_width = gathered.shape
    query_width = w_query.shape[1]
    keyval_width = w_keyval.shape[1]
    kept_rows = row_total // lax.axis_size("gx")
    row_block = gathered.reshape(lax.axis_size("gx") * kept_rows * step_total, local_width)
    query_term = jnp.dot(row_block, w_query, preferred_element_type=jnp.float32).reshape(
        lax.axis_size("gx") * kept_rows, step_total, query_width
    )
    keyval_term = jnp.dot(row_block, w_keyval, preferred_element_type=jnp.float32).reshape(
        lax.axis_size("gx") * kept_rows, step_total, keyval_width
    )
    summed = lax.psum_scatter(
        jnp.concatenate((query_term, keyval_term), axis=2), "gx", scatter_dimension=0, tiled=True
    ).astype(jnp.bfloat16)
    queries, keyvals = (
        lax.all_to_all(summed[:, :, :query_width], "gy", split_axis=0, concat_axis=2, tiled=True),
        lax.all_to_all(summed[:, :, query_width:], "gy", split_axis=0, concat_axis=2, tiled=True),
    )
    return (queries, keyvals)


def attend(queries, keyvals, cache_key, cache_value, lengths):
    sequences, step_total, row_width = queries.shape
    head_dim = cache_key.shape[2]
    head_count = row_width // head_dim
    cache_len = cache_key.shape[1]
    inverse_root = head_dim ** (-0.5)
    flat_queries = queries.reshape(sequences, step_total * head_count, head_dim)
    draft_keys = keyvals[:, :, :head_dim]
    draft_values = keyvals[:, :, head_dim:]
    draft_scores = (
        jnp.einsum("sqd,sud->squ", flat_queries, draft_keys, preferred_element_type=jnp.float32)
        * inverse_root
    )
    query_step = (
        lax.broadcasted_iota(jnp.int32, (step_total * head_count, step_total), 0) // head_count
    )
    draft_step = lax.broadcasted_iota(jnp.int32, (step_total * head_count, step_total), 1)
    draft_allowed = (draft_step <= query_step)[None]
    draft_scores = jnp.where(draft_allowed, draft_scores, -1e30)
    highest = jnp.max(draft_scores, axis=-1)
    scores = (
        jnp.einsum("sqd,spd->sqp", flat_queries, cache_key, preferred_element_type=jnp.float32)
        * inverse_root
    )
    positions = lax.broadcasted_iota(jnp.int32, (1, 1, cache_len), 2)
    allowed = positions < lengths[:, None, None]
    scores = jnp.where(allowed, scores, -1e30)
    highest = jnp.maximum(highest, jnp.max(scores, axis=-1))
    weights = jnp.where(allowed, jnp.exp(scores - highest[..., None]), 0.0)
    denominator = jnp.sum(weights, axis=-1)
    summed = jnp.einsum(
        "sqp,spd->sqd",
        weights.astype(jnp.bfloat16),
        cache_value,
        preferred_element_type=jnp.float32,
    )
    draft_weights = jnp.where(draft_allowed, jnp.exp(draft_scores - highest[..., None]), 0.0)
    denominator = denominator + jnp.sum(draft_weights, axis=-1)
    summed = summed + jnp.einsum(
        "squ,sud->sqd",
        draft_weights.astype(jnp.bfloat16),
        draft_values,
        preferred_element_type=jnp.float32,
    )
    return (
        (summed / denominator[..., None])
        .astype(jnp.bfloat16)
        .reshape(sequences, step_total, row_width)
    )


def on_device(tokens, norm_gain, w_query, w_keyval, cache_keys, cache_values, lengths):
    inputs = tokens[0]
    step_total = inputs.shape[1]
    per_round = 1
    query_parts = []
    keyval_parts = []
    for begin_step in range(0, step_total, per_round):
        normed = normalize(inputs[:, begin_step : begin_step + per_round], norm_gain)
        queries, keyvals = project(normed, w_query, w_keyval)
        query_parts.append(queries)
        keyval_parts.append(keyvals)
    queries = jnp.concatenate(query_parts, axis=1)
    keyvals = jnp.concatenate(keyval_parts, axis=1)
    attended = attend(queries, keyvals, cache_keys[0], cache_values[0], lengths[0])
    return (attended[None], keyvals[None])


def solution(mesh):
    return jax.shard_map(
        on_device,
        mesh=mesh,
        in_specs=(
            P("gz", "gy", None, "gx"),
            P("gx"),
            P("gx", "gy"),
            P("gx", "gy"),
            P("gz", ("gx", "gy"), None, None),
            P("gz", ("gx", "gy"), None, None),
            P("gz", ("gx", "gy")),
        ),
        out_specs=(P("gz", ("gx", "gy"), None, None), P("gz", ("gx", "gy"), None, None)),
        check_vma=False,
    )
```

profile of v0, /device:TPU:0, one launch (start us, length us, event | category | flops | bytes accessed | tf_op | source)
XLA Modules:
  0.0 236.4 jit_solution(13786139045855075847)
XLA Ops:
  0.6 0.0 copy-start
  0.6 1.0 copy.28
  1.7 0.2 convert_reduce_fusion.3
  1.9 23.1 %all-reduce.5 = (f32[8,1]{0,1:T(1,128)S(1)}, f32[8,1]{0,1:T(1,128)S(1)}, f32[8,1]{0,1:T(1,128)S(1)}, f32[8,1]{0,1:T(1,128)S(1)}, f32[8,1]{0,1:T(1,128)S(1)}, /*i...) all-reduce(f32[8,1]{0,1:T(1,128)S(1)} %bitcast.120, ...), channel_id=1, replica_groups=mesh['gx'=8,'gy'=2,'gz'=2] {'gx'}, use_global_device_ids=true, to_apply=%region_18.0 | all-reduce | flops 64 | bytes 512 | tf_op jit(solution)/shard_map/psum | solution.py:11
  25.1 0.8 fusion.15
  25.9 4.6 %all_gather.12 = bf16[16,1,2304]{2,0,1:T(8,128)(2,1)S(1)} all-gather(bf16[8,1,2304]{2,0,1:T(8,128)(2,1)S(1)} %get-tuple-element.22), channel_id=1, replica_groups=mesh['gx'=8,'gy'=2,'gz'=2] {'gy'}, dimensions={0}, use_global_device_ids=true | all-gather | bytes 110592 | tf_op jit(solution)/shard_map/all_gather | solution.py:21
  30.5 11.0 %convolution_bitcast_fusion.3 = f32[16,1,6144]{2,0,1:T(8,128)S(1)} fusion(bf16[2304,6144]{1,0:T(8,128)(2,1)} %param.9, bf16[16,1,2304]{2,0,1:T(8,128)(2,1)S(1)} %all_gather.12), kind=kOutput, calls=%fused_computation.5 | convolution fusion | flops 452984832 | bytes 28778496 | tf_op jit(solution)/shard_map/dot_general | solution.py:27
  41.5 0.2 convolution_bitcast_fusion.7
  41.8 4.7 %all_gather.13 = bf16[16,1,2304]{2,0,1:T(8,128)(2,1)S(1)} all-gather(bf16[8,1,2304]{2,0,1:T(8,128)(2,1)S(1)} %get-tuple-element.23), channel_id=1, replica_groups=mesh['gx'=8,'gy'=2,'gz'=2] {'gy'}, dimensions={0}, use_global_device_ids=true | all-gather | bytes 110592 | tf_op jit(solution)/shard_map/all_gather | solution.py:21
  46.4 11.0 %convolution_bitcast_fusion.2 = f32[16,1,6144]{2,0,1:T(8,128)S(1)} fusion(bf16[2304,6144]{1,0:T(8,128)(2,1)} %param.9, bf16[16,1,2304]{2,0,1:T(8,128)(2,1)S(1)} %all_gather.13), kind=kOutput, calls=%fused_computation.4 | convolution fusion | flops 452984832 | bytes 28778496 | tf_op jit(solution)/shard_map/dot_general | solution.py:27
  57.4 0.2 convolution_bitcast_fusion.6
  57.7 4.7 %all_gather.14 = bf16[16,1,2304]{2,0,1:T(8,128)(2,1)S(1)} all-gather(bf16[8,1,2304]{2,0,1:T(8,128)(2,1)S(1)} %get-tuple-element.24), channel_id=1, replica_groups=mesh['gx'=8,'gy'=2,'gz'=2] {'gy'}, dimensions={0}, use_global_device_ids=true | all-gather | bytes 110592 | tf_op jit(solution)/shard_map/all_gather | solution.py:21
  62.3 11.0 %convolution_bitcast_fusion.1 = f32[16,1,6144]{2,0,1:T(8,128)S(1)} fusion(bf16[2304,6144]{1,0:T(8,128)(2,1)} %param.9, bf16[16,1,2304]{2,0,1:T(8,128)(2,1)S(1)} %all_gather.14), kind=kOutput, calls=%fused_computation.3 | convolution fusion | flops 452984832 | bytes 28778496 | tf_op jit(solution)/shard_map/dot_general | solution.py:27
  73.3 0.2 convolution_bitcast_fusion.5
  73.6 4.7 %all_gather.15 = bf16[16,1,2304]{2,0,1:T(8,128)(2,1)S(1)} all-gather(bf16[8,1,2304]{2,0,1:T(8,128)(2,1)S(1)} %get-tuple-element.25), channel_id=1, replica_groups=mesh['gx'=8,'gy'=2,'gz'=2] {'gy'}, dimensions={0}, use_global_device_ids=true | all-gather | bytes 110592 | tf_op jit(solution)/shard_map/all_gather | solution.py:21
  78.3 11.0 %convolution_bitcast_fusion = f32[16,1,6144]{2,0,1:T(8,128)S(1)} fusion(bf16[2304,6144]{1,0:T(8,128)(2,1)} %param.9, bf16[16,1,2304]{2,0,1:T(8,128)(2,1)S(1)} %all_gather.15), kind=kOutput, calls=%fused_computation.2 | convolution fusion | flops 452984832 | bytes 28778496 | tf_op jit(solution)/shard_map/dot_general | solution.py:27
  89.3 0.2 convolution_bitcast_fusion.4
  89.5 0.1 pad_maximum_fusion
  89.7 0.6 dynamic-slice
  91.0 78.4 %all-reduce.7 = (bf16[16,1,6400]{2,0,1:T(8,128)(2,1)S(1)}, bf16[16,1,6400]{2,0,1:T(8,128)(2,1)S(1)}, bf16[16,1,6400]{2,0,1:T(8,128)(2,1)S(1)}, bf16[16,1,6400]{2,0,1:T(8,128)(2,1)}) all-reduce(f32[16,1,6400]{2,0,1:T(8,128)S(1)} %pad_maximum_fusion.3, ...), channel_id=5, replica_groups=mesh['gx'=8,'gy'=2,'gz'=2] {'gx'}, use_global_device_ids=true, to_apply=%region_19.0.clone | all-reduce | flops 409600 | bytes 2457600
  169.4 0.9 dynamic-slice_convert_fusion.3
  170.3 0.5 broadcast.73
  170.8 0.6 reduce.23
  171.5 0.6 reshape.227
  172.1 3.2 %all-to-all-start.4 = ((bf16[2,2,128]{2,1,0:T(2,128)(2,1)}), bf16[2,2,128]{2,1,0:T(2,128)(2,1)S(1)}, u32[]{:S(2)}, u32[]{:S(2)}) async-start(bf16[2,2,128]{2,1,0:T(2,128)(2,1)} %reshape.227), calls=%async_computation.4 | async-start | bytes 2048 | tf_op jit(solution)/shard_map/all_to_all | solution.py:38
  175.3 0.6 reduce.22
  176.0 0.6 reshape.225
  176.5 2.4 %all-to-all-done.4 = bf16[2,2,128]{2,1,0:T(2,128)(2,1)S(1)} async-done(((bf16[2,2,128]{2,1,0:T(2,128)(2,1)}), bf16[2,2,128]{2,1,0:T(2,128)(2,1)S(1)}, u32[]{:S(2)}, u32[]{:S(2)}) %all-to-all-start.4) | async-done | bytes 1056 | tf_op jit(solution)/shard_map/all_to_all | solution.py:38
  178.9 3.2 %all-to-all-start.5 = ((bf16[2,2,128]{2,1,0:T(2,128)(2,1)}), bf16[2,2,128]{2,1,0:T(2,128)(2,1)S(1)}, u32[]{:S(2)}, u32[]{:S(2)}) async-start(bf16[2,2,128]{2,1,0:T(2,128)(2,1)} %reshape.225), calls=%async_computation.5 | async-start | bytes 2048 | tf_op jit(solution)/shard_map/all_to_all | solution.py:38
  182.2 0.6 reduce.21
  182.8 0.6 reshape.223
  183.4 2.4 %all-to-all-done.5 = bf16[2,2,128]{2,1,0:T(2,128)(2,1)S(1)} async-done(((bf16[2,2,128]{2,1,0:T(2,128)(2,1)}), bf16[2,2,128]{2,1,0:T(2,128)(2,1)S(1)}, u32[]{:S(2)}, u32[]{:S(2)}) %all-to-all-start.5) | async-done | bytes 1056 | tf_op jit(solution)/shard_map/all_to_all | solution.py:38
  185.8 3.2 %all-to-all-start.6 = ((bf16[2,2,128]{2,1,0:T(2,128)(2,1)}), bf16[2,2,128]{2,1,0:T(2,128)(2,1)S(1)}, u32[]{:S(2)}, u32[]{:S(2)}) async-start(bf16[2,2,128]{2,1,0:T(2,128)(2,1)} %reshape.223), calls=%async_computation.6 | async-start | bytes 2048 | tf_op jit(solution)/shard_map/all_to_all | solution.py:38
  189.0 0.6 reduce.20
  189.7 0.6 reshape.221
  190.9 1.7 all-to-all-done.6
  192.6 3.2 %all-to-all-start.7 = ((bf16[2,2,128]{2,1,0:T(2,128)(2,1)}), bf16[2,2,128]{2,1,0:T(2,128)(2,1)S(1)}, u32[]{:S(2)}, u32[]{:S(2)}) async-start(bf16[2,2,128]{2,1,0:T(2,128)(2,1)} %reshape.221), calls=%async_computation.7 | async-start | bytes 2048 | tf_op jit(solution)/shard_map/all_to_all | solution.py:38
  195.9 0.7 reduce.18
  196.6 0.6 reshape.217
  197.2 2.3 all-to-all-done.7
  199.5 3.2 %all-to-all-start.1 = ((bf16[2,2,3072]{2,1,0:T(2,128)(2,1)}), bf16[2,2,3072]{2,1,0:T(2,128)(2,1)S(1)}, u32[]{:S(2)}, u32[]{:S(2)}) async-start(bf16[2,2,3072]{2,1,0:T(2,128)(2,1)} %reshape.217), calls=%async_computation.1 | async-start | bytes 49152 | tf_op jit(solution)/shard_map/all_to_all | solution.py:37
  202.8 0.7 reduce.17
  203.5 0.6 reshape.215
  204.1 2.5 %all-to-all-done.1 = bf16[2,2,3072]{2,1,0:T(2,128)(2,1)S(1)} async-done(((bf16[2,2,3072]{2,1,0:T(2,128)(2,1)}), bf16[2,2,3072]{2,1,0:T(2,128)(2,1)S(1)}, u32[]{:S(2)}, u32[]{:S(2)}) %all-to-all-start.1) | async-done | bytes 24608 | tf_op jit(solution)/shard_map/all_to_all | solution.py:37
  206.6 3.2 %all-to-all-start.2 = ((bf16[2,2,3072]{2,1,0:T(2,128)(2,1)}), bf16[2,2,3072]{2,1,0:T(2,128)(2,1)S(1)}, u32[]{:S(2)}, u32[]{:S(2)}) async-start(bf16[2,2,3072]{2,1,0:T(2,128)(2,1)} %reshape.215), calls=%async_computation.2 | async-start | bytes 49152 | tf_op jit(solution)/shard_map/all_to_all | solution.py:37
  210.0 0.7 reduce.16
  210.6 0.6 reshape.213
  211.3 0.7 reduce.19
  212.0 0.6 reshape.219
  212.6 1.1 all-to-all-done.2
  213.8 3.2 %all-to-all-start.3 = ((bf16[2,2,3072]{2,1,0:T(2,128)(2,1)}), bf16[2,2,3072]{2,1,0:T(2,128)(2,1)S(1)}, u32[]{:S(2)}, u32[]{:S(2)}) async-start(bf16[2,2,3072]{2,1,0:T(2,128)(2,1)} %reshape.213), calls=%async_computation.3 | async-start | bytes 49152 | tf_op jit(solution)/shard_map/all_to_all | solution.py:37
  217.0 0.6 fusion.52
  217.6 3.3 %all-to-all-done.3 = bf16[2,2,3072]{2,1,0:T(2,128)(2,1)S(1)} async-done(((bf16[2,2,3072]{2,1,0:T(2,128)(2,1)}), bf16[2,2,3072]{2,1,0:T(2,128)(2,1)S(1)}, u32[]{:S(2)}, u32[]{:S(2)}) %all-to-all-start.3) | async-done | bytes 24608 | tf_op jit(solution)/shard_map/all_to_all | solution.py:37
  220.9 3.4 %all-to-all-start = ((bf16[2,2,3072]{2,1,0:T(2,128)(2,1)}), bf16[2,2,3072]{2,1,0:T(2,128)(2,1)S(1)}, u32[]{:S(2)}, u32[]{:S(2)}) async-start(bf16[2,2,3072]{2,1,0:T(2,128)(2,1)} %reshape.219), calls=%async_computation | async-start | bytes 49152 | tf_op jit(solution)/shard_map/all_to_all | solution.py:37
  224.5 3.6 %all-to-all-done = bf16[2,2,3072]{2,1,0:T(2,128)(2,1)S(1)} async-done(((bf16[2,2,3072]{2,1,0:T(2,128)(2,1)}), bf16[2,2,3072]{2,1,0:T(2,128)(2,1)S(1)}, u32[]{:S(2)}, u32[]{:S(2)}) %all-to-all-start) | async-done | bytes 24608 | tf_op jit(solution)/shard_map/all_to_all | solution.py:37
  228.1 0.2 pad_maximum_fusion.4
  228.4 3.8 %fusion.41 = (f32[192]{0:T(256)S(1)}, f32[192,8192]{1,0:T(8,128)S(1)}) fusion(bf16[192,256]{1,0:T(8,128)(2,1)S(1)} %reshape.196, bf16[1,1,8192,256]{3,2,1,0:T(8,128)(2,1)} %param.11, pred[8192]{0:T(1024)(128)(4,1)S(1)} %iota_compare_fusion), kind=kOutput, calls=%fused_computation.93 | convolution fusion | flops 810024768 | bytes 10593024 | tf_op jit(solution)/shard_map/sqd,spd->sqp/dot_general | solution.py:64
  232.2 0.0 copy-start.1
  232.2 0.2 fusion.40
  232.4 1.4 fusion.1
  233.8 0.6 copy-done.1
  234.4 1.0 fusion.3
  235.5 0.2 fusion.11
  235.7 0.7 broadcast_in_dim_reshape.3
  (35 shorter events, 0.6 us)
Async XLA Ops:
  0.6 40.9 %copy-start = (bf16[2304,256]{1,0:T(8,128)(2,1)S(1)}, bf16[2304,256]{1,0:T(8,128)(2,1)}, u32[]{:S(2)}) copy-start(bf16[2304,256]{1,0:T(8,128)(2,1)} %param.10) | copy-start | bytes 3538948
  78.3 11.5 %copy-start.2 = (u32[32]{0:T(128)S(1)}, u32[32]{0:T(128)}, u32[]{:S(2)}) copy-start(u32[32]{0:T(128)} %constant.38) | copy-start | bytes 388
  172.1 6.9 %all-to-all-start.4 = ((bf16[2,2,128]{2,1,0:T(2,128)(2,1)}), bf16[2,2,128]{2,1,0:T(2,128)(2,1)S(1)}, u32[]{:S(2)}, u32[]{:S(2)}) async-start(bf16[2,2,128]{2,1,0:T(2,128)(2,1)} %reshape.227), calls=%async_computation.4 | async-start | bytes 2048 | tf_op jit(solution)/shard_map/all_to_all | solution.py:38
  178.9 6.9 %all-to-all-start.5 = ((bf16[2,2,128]{2,1,0:T(2,128)(2,1)}), bf16[2,2,128]{2,1,0:T(2,128)(2,1)S(1)}, u32[]{:S(2)}, u32[]{:S(2)}) async-start(bf16[2,2,128]{2,1,0:T(2,128)(2,1)} %reshape.225), calls=%async_computation.5 | async-start | bytes 2048 | tf_op jit(solution)/shard_map/all_to_all | solution.py:38
  185.8 6.9 %all-to-all-start.6 = ((bf16[2,2,128]{2,1,0:T(2,128)(2,1)}), bf16[2,2,128]{2,1,0:T(2,128)(2,1)S(1)}, u32[]{:S(2)}, u32[]{:S(2)}) async-start(bf16[2,2,128]{2,1,0:T(2,128)(2,1)} %reshape.223), calls=%async_computation.6 | async-start | bytes 2048 | tf_op jit(solution)/shard_map/all_to_all | solution.py:38
  192.6 6.9 %all-to-all-start.7 = ((bf16[2,2,128]{2,1,0:T(2,128)(2,1)}), bf16[2,2,128]{2,1,0:T(2,128)(2,1)S(1)}, u32[]{:S(2)}, u32[]{:S(2)}) async-start(bf16[2,2,128]{2,1,0:T(2,128)(2,1)} %reshape.221), calls=%async_computation.7 | async-start | bytes 2048 | tf_op jit(solution)/shard_map/all_to_all | solution.py:38
  199.5 7.1 %all-to-all-start.1 = ((bf16[2,2,3072]{2,1,0:T(2,128)(2,1)}), bf16[2,2,3072]{2,1,0:T(2,128)(2,1)S(1)}, u32[]{:S(2)}, u32[]{:S(2)}) async-start(bf16[2,2,3072]{2,1,0:T(2,128)(2,1)} %reshape.217), calls=%async_computation.1 | async-start | bytes 49152 | tf_op jit(solution)/shard_map/all_to_all | solution.py:37
  206.6 7.1 %all-to-all-start.2 = ((bf16[2,2,3072]{2,1,0:T(2,128)(2,1)}), bf16[2,2,3072]{2,1,0:T(2,128)(2,1)S(1)}, u32[]{:S(2)}, u32[]{:S(2)}) async-start(bf16[2,2,3072]{2,1,0:T(2,128)(2,1)} %reshape.215), calls=%async_computation.2 | async-start | bytes 49152 | tf_op jit(solution)/shard_map/all_to_all | solution.py:37
  213.8 7.1 %all-to-all-start.3 = ((bf16[2,2,3072]{2,1,0:T(2,128)(2,1)}), bf16[2,2,3072]{2,1,0:T(2,128)(2,1)S(1)}, u32[]{:S(2)}, u32[]{:S(2)}) async-start(bf16[2,2,3072]{2,1,0:T(2,128)(2,1)} %reshape.213), calls=%async_computation.3 | async-start | bytes 49152 | tf_op jit(solution)/shard_map/all_to_all | solution.py:37
  220.9 7.1 %all-to-all-start = ((bf16[2,2,3072]{2,1,0:T(2,128)(2,1)}), bf16[2,2,3072]{2,1,0:T(2,128)(2,1)S(1)}, u32[]{:S(2)}, u32[]{:S(2)}) async-start(bf16[2,2,3072]{2,1,0:T(2,128)(2,1)} %reshape.219), calls=%async_computation | async-start | bytes 49152 | tf_op jit(solution)/shard_map/all_to_all | solution.py:37
  232.2 2.2 copy-start.1
where the time goes:
time: 237 us; the launch traced here: 236 us
  blocking collectives  120 us (51%)
  matrix products  50.2 us (21%)
  starting transfers between devices  25.9 us (11%)
  waiting for transfers between devices  19.3 us (8%)
  local copies, waits for them, and re-layouts  9.57 us (4%)
  other arithmetic  8.9 us (4%)
    unnamed x1, blocking collectives  78.4 us
    dot_general x4, matrix products, project(): jnp.dot(row_block, w_query, preferred_element_type=jnp.float32)  44 us
    psum x1, blocking collectives, normalize(): lax.psum((jnp.sum(values, axis=-1), jnp.sum(values * values, axis=-1)), '...  23.1 us
    all_gather x4, blocking collectives, project(): gathered = lax.all_gather(normed, 'gy', axis=0, tiled=True)  18.6 us
    all_to_all x4, starting transfers between devices, project(): lax.all_to_all(summed[:, :, :query_width], 'gy', split_axis=0, concat_axi...  13.2 us
    all_to_all x4, starting transfers between devices, project(): lax.all_to_all(summed[:, :, query_width:], 'gy', split_axis=0, concat_axi...  12.8 us
    all_to_all x4, waiting for transfers between devices, project(): lax.all_to_all(summed[:, :, :query_width], 'gy', split_axis=0, concat_axi...  10.6 us
    all_to_all x4, waiting for transfers between devices, project(): lax.all_to_all(summed[:, :, query_width:], 'gy', split_axis=0, concat_axi...  8.76 us
  transfers between devices with their start and end apart: 8, of which 8 were waited for; matrix products, arithmetic and copies ran while one was open for 4% of the time, Pallas kernels for 0%

commit v1 on v0

v1 whole, which is shorter than its diff:
```python
import functools
import math

import jax
import jax.numpy as jnp
from jax import lax
from jax.experimental import pallas as pl
from jax.experimental.pallas import tpu as pltpu
from jax.sharding import PartitionSpec as P

D = 18432
HD = 256
OUTER = 4
LANES = 128
PACK = 16
MESH = pl.DeviceIdType.MESH


def project_kernel(
    sizes,
    x_ref,
    gain_ref,
    wq_hbm,
    wkv_hbm,
    out_ref,
    wq,
    wkv,
    rows,
    stat_send,
    stat_recv,
    product,
    a_send,
    a_recv,
    kept,
    b_send,
    b_recv,
    own,
    c_send,
    c_recv,
    w_sem,
    st_ssem,
    st_rsem,
    y_ssem,
    y_rsem,
    k_ssem,
    k_rsem,
    a_ssem,
    a_rsem,
    b_ssem,
    b_rsem,
    c_ssem,
    c_rsem,
):
    X, Y, Z, seqs, steps = sizes
    NZ = OUTER
    NX = X // NZ
    G = Y * Z
    block = seqs * steps
    group = Y * steps
    per_block = seqs // Y
    dest_rows = Z * group
    query_half = wq.shape[1]
    keyval_half = wkv.shape[1]
    width = a_send.shape[-1]
    query_chunks = query_half // width
    chunks = query_chunks + 1

    i = lax.axis_index("gx")
    j = lax.axis_index("gy")
    k = lax.axis_index("gz")
    zi = i // NX
    xi = i % NX
    me = j * Z + k

    def chunk_width(c):
        return width if c < query_chunks else keyval_half

    def query_load(c):
        begin = pl.multiple_of(k * query_half + c * width, LANES)
        return pltpu.make_async_copy(
            wq_hbm.at[:, pl.ds(begin, width)],
            wq.at[:, pl.ds(c * width, width)],
            w_sem.at[c],
        )

    keyval_load = pltpu.make_async_copy(
        wkv_hbm.at[:, pl.ds(pl.multiple_of(k * keyval_half, LANES), keyval_half)],
        wkv,
        w_sem.at[query_chunks],
    )
    loads = [query_load(c) for c in range(query_chunks)] + [keyval_load]
    for load in loads:
        load.start()

    barrier = pltpu.get_barrier_semaphore()
    for d in range(1, X):
        pl.semaphore_signal(
            barrier, inc=1, device_id={"gx": (i + d) % X, "gy": j, "gz": k}, device_id_type=MESH
        )
    for dj in range(Y):
        for dk in range(Z):
            if dj or dk:
                pl.semaphore_signal(
                    barrier,
                    inc=1,
                    device_id={"gx": i, "gy": (j + dj) % Y, "gz": (k + dk) % Z},
                    device_id_type=MESH,
                )

    values = x_ref[...].astype(jnp.float32)
    row_sum = jnp.sum(values, axis=1, keepdims=True)
    row_square = jnp.sum(values * values, axis=1, keepdims=True)
    lane = lax.broadcasted_iota(jnp.int32, (block, LANES), 1)
    packed = jnp.where(lane == 0, row_sum, jnp.where(lane == 1, row_square, 0.0))
    packed = jnp.concatenate(
        (packed, jnp.zeros((LANES - block, LANES), jnp.float32)), axis=0
    )
    stat_send[...] = packed.T[:8]

    pl.semaphore_wait(barrier, X - 1 + G - 1)

    sends = []

    def send(src, dst, ssem, rsem, di, dj, dk):
        copy = pltpu.make_async_remote_copy(
            src_ref=src,
            dst_ref=dst,
            send_sem=ssem,
            recv_sem=rsem,
            device_id={"gx": di, "gy": dj, "gz": dk},
            device_id_type=MESH,
        )
        copy.start()
        sends.append(copy)
        return copy

    stat_copies = [
        send(stat_send, stat_recv.at[d], st_ssem.at[d], st_rsem.at[d], (i + d) % X, j, k)
        for d in range(1, X)
    ]
    total = stat_send[...]
    for d in range(1, X):
        stat_copies[d - 1].wait_recv()
        total = total + stat_recv[d]
    total = jnp.concatenate((total, jnp.zeros((LANES - 8, LANES), jnp.float32)), axis=0).T
    center = total[:block, 0:1] / D
    spread = total[:block, 1:2] / D - center * center
    factor = lax.rsqrt(spread + 1e-05)
    normed = ((x_ref[...].astype(jnp.float32) - center) * factor * gain_ref[...]).astype(jnp.bfloat16)
    own_rows = pl.ds(pl.multiple_of(me * block, block), block)
    rows[own_rows, :] = normed

    def row_block(dj):
        g = ((j + Y - dj) % Y) * Z + k
        return rows.at[pl.ds(pl.multiple_of(g * block, block), block), :]

    y_copies = [None] + [
        send(row_block(0), row_block(0), y_ssem.at[dj], y_rsem.at[dj], i, (j + dj) % Y, k)
        for dj in range(1, Y)
    ]
    k_copies = []
    for dj in range(Y):
        if dj:
            y_copies[dj].wait_recv()
        for dk in range(1, Z):
            k_copies.append(
                send(
                    row_block(dj),
                    row_block(dj),
                    k_ssem.at[dj, dk],
                    k_rsem.at[dj, dk],
                    i,
                    j,
                    (k + dk) % Z,
                )
            )
    for copy in k_copies:
        copy.wait_recv()

    def multiply(c):
        loads[c].wait()
        if c < query_chunks:
            tile = HD

            def body(n, carry):
                here = pl.ds(pl.multiple_of(n * tile, tile), tile)
                there = pl.ds(pl.multiple_of(c * width + n * tile, tile), tile)
                product[:, here] = jnp.dot(
                    rows[...], wq[:, there], preferred_element_type=jnp.float32
                )
                return carry

            lax.fori_loop(0, width // tile, body, 0)
        else:
            product[:, :keyval_half] = jnp.dot(
                rows[...], wkv[...], preferred_element_type=jnp.float32
            )

    def rows_for(di, dk, w):
        g = (di // per_block) * Z + dk
        begin = pl.multiple_of(g * block + (di % per_block) * group, group)
        return product[pl.ds(begin, group), :w]

    a_copies = {}
    b_copies = {}
    c_copies = {}

    def stage_a(c):
        w = chunk_width(c)
        for dx in range(1, NX):
            to_x = (xi + dx) % NX
            for z in range(NZ):
                part = jnp.concatenate(
                    [rows_for(z * NX + to_x, dk, w) for dk in range(Z)], axis=0
                )
                a_send[c, dx, z * dest_rows : (z + 1) * dest_rows, :w] = part.astype(jnp.bfloat16)
            a_copies[c, dx] = send(
                a_send.at[c, dx, :, :w],
                a_recv.at[c, dx, :, :w],
                a_ssem.at[c, dx],
                a_rsem.at[c, dx],
                zi * NX + to_x,
                j,
                k,
            )
        for z in range(NZ):
            kept[c, z, :, :w] = jnp.concatenate(
                [rows_for(z * NX + xi, dk, w) for dk in range(Z)], axis=0
            )

    def stage_b(c):
        w = chunk_width(c)
        for dx in range(1, NX):
            a_copies[c, dx].wait_recv()
        for z in range(NZ):
            part = kept[c, z, :, :w]
            for dx in range(1, NX):
                part = part + a_recv[
                    c, dx, z * dest_rows : (z + 1) * dest_rows, :w
                ].astype(jnp.float32)
            kept[c, z, :, :w] = part
            b_send[c, z, :, :w] = part.astype(jnp.bfloat16)
        for dz in range(1, NZ):
            to_z = (zi + dz) % NZ
            b_copies[c, dz] = send(
                b_send.at[c, to_z, :, :w],
                b_recv.at[c, dz, :, :w],
                b_ssem.at[c, dz],
                b_rsem.at[c, dz],
                to_z * NX + xi,
                j,
                k,
            )
        own[c, :, :w] = kept[c, zi, :, :w]

    def stage_c(c):
        w = chunk_width(c)
        part = own[c, :, :w]
        for dz in range(1, NZ):
            b_copies[c, dz].wait_recv()
            part = part + b_recv[c, dz, :, :w].astype(jnp.float32)
        for dj in range(Y):
            for dk in range(Z):
                begin = (dk * Y + dj) * steps
                mine = part[begin : begin + steps, :]
                if w < HD:
                    mine = jnp.concatenate(
                        (mine, jnp.zeros((steps, HD - w), jnp.float32)), axis=1
                    )
                pieces = [mine[:, h * HD : (h + 1) * HD] for h in range(mine.shape[1] // HD)]
                missing = PACK - steps * len(pieces)
                if missing:
                    pieces.append(jnp.zeros((missing, HD), jnp.float32))
                c_send[c, dj * Z + dk] = jnp.concatenate(pieces, axis=0).astype(jnp.bfloat16)
        for dj in range(Y):
            for dk in range(Z):
                if dj or dk:
                    to_j = (j + dj) % Y
                    to_k = (k + dk) % Z
                    slot = dj * Z + dk
                    c_copies[c, slot] = send(
                        c_send.at[c, to_j * Z + to_k],
                        c_recv.at[c, me],
                        c_ssem.at[c, slot],
                        c_rsem.at[c, slot],
                        i,
                        to_j,
                        to_k,
                    )
        c_recv[c, me] = c_send[c, me]

    for c in range(chunks + 2):
        if c < chunks:
            multiply(c)
            stage_a(c)
        if 1 <= c < chunks + 1:
            stage_b(c - 1)
        if 2 <= c:
            stage_c(c - 2)
    for copy in c_copies.values():
        copy.wait_recv()
    out_ref[...] = c_recv[...]
    for copy in sends:
        copy.wait_send()


def project(tokens, gain, w_query, w_keyval):
    X, Y, Z = lax.axis_size("gx"), lax.axis_size("gy"), lax.axis_size("gz")
    seqs, steps, depth = tokens.shape
    G = Y * Z
    NZ = OUTER
    NX = X // NZ
    block = seqs * steps
    dest_rows = Z * Y * steps
    query_half = w_query.shape[1] // Z
    keyval_half = w_keyval.shape[1] // Z
    width = min(query_half, HD * (PACK // steps))
    chunks = query_half // width + 1
    bf16, f32 = jnp.bfloat16, jnp.float32
    any_space = pl.BlockSpec(memory_space=pl.ANY)
    vmem = pl.BlockSpec(memory_space=pltpu.VMEM)
    dma = pltpu.SemaphoreType.DMA
    return pl.pallas_call(
        functools.partial(project_kernel, (X, Y, Z, seqs, steps)),
        out_shape=jax.ShapeDtypeStruct((chunks, G, PACK, HD), bf16),
        in_specs=[vmem, vmem, any_space, any_space],
        out_specs=vmem,
        scratch_shapes=[
            pltpu.VMEM((depth, query_half), bf16),
            pltpu.VMEM((depth, keyval_half), bf16),
            pltpu.VMEM((G * block, depth), bf16),
            pltpu.VMEM((8, LANES), f32),
            pltpu.VMEM((X, 8, LANES), f32),
            pltpu.VMEM((G * block, width), f32),
            pltpu.VMEM((chunks, NX, NZ * dest_rows, width), bf16),
            pltpu.VMEM((chunks, NX, NZ * dest_rows, width), bf16),
            pltpu.VMEM((chunks, NZ, dest_rows, width), f32),
            pltpu.VMEM((chunks, NZ, dest_rows, width), bf16),
            pltpu.VMEM((chunks, NZ, dest_rows, width), bf16),
            pltpu.VMEM((chunks, dest_rows, width), f32),
            pltpu.VMEM((chunks, G, PACK, HD), bf16),
            pltpu.VMEM((chunks, G, PACK, HD), bf16),
            dma((chunks,)),
            dma((X,)),
            dma((X,)),
            dma((Y,)),
            dma((Y,)),
            dma((Y, Z)),
            dma((Y, Z)),
            dma((chunks, NX)),
            dma((chunks, NX)),
            dma((chunks, NZ)),
            dma((chunks, NZ)),
            dma((chunks, G)),
            dma((chunks, G)),
        ],
        compiler_params=pltpu.CompilerParams(
            collective_id=0, has_side_effects=True, vmem_limit_bytes=56 * 2**20
        ),
        cost_estimate=pl.CostEstimate(
            flops=2 * G * block * depth * (query_half + keyval_half),
            bytes_accessed=2 * depth * (query_half + keyval_half),
            transcendentals=0,
        ),
    )(tokens.reshape(block, depth), gain.reshape(1, depth), w_query, w_keyval)


def attend_kernel(sizes, len_ref, q_ref, k_ref, v_ref, out_ref, new_ref, acc, top, total):
    heads, steps, keyval_real = sizes
    chunks, G = q_ref.shape[0] - 1, q_ref.shape[1]
    query_rows = chunks * G * PACK
    scale = HD**-0.5 * math.log2(math.e)
    p = pl.program_id(0)
    span = k_ref.shape[0]
    queries = q_ref[:chunks].reshape(query_rows, HD)
    transposed = (((1,), (1,)), ((), ()))

    @pl.when(p == 0)
    def _():
        entries = jnp.concatenate(
            [q_ref[chunks, g, :, :keyval_real] for g in range(G)], axis=1
        )
        new_ref[...] = entries[:steps]
        scores = scale * lax.dot_general(
            queries, entries[:, :HD], transposed, preferred_element_type=jnp.float32
        )
        row_step = lax.broadcasted_iota(jnp.int32, scores.shape, 0) % steps
        entry_step = lax.broadcasted_iota(jnp.int32, scores.shape, 1)
        scores = jnp.where(entry_step <= row_step, scores, -1e30)
        highest = jnp.max(scores, axis=1, keepdims=True)
        weights = jnp.exp2(scores - highest)
        top[...] = jnp.broadcast_to(highest, top.shape)
        total[...] = jnp.broadcast_to(jnp.sum(weights, axis=1, keepdims=True), total.shape)
        acc[...] = jnp.dot(
            weights.astype(jnp.bfloat16), entries[:, HD:], preferred_element_type=jnp.float32
        )

    scores = scale * lax.dot_general(
        queries, k_ref[...], transposed, preferred_element_type=jnp.float32
    )
    position = p * span + lax.broadcasted_iota(jnp.int32, (1, span), 1)
    scores = jnp.where(position < len_ref[0, 0], scores, -1e30)
    before = top[:, :1]
    highest = jnp.maximum(before, jnp.max(scores, axis=1, keepdims=True))
    weights = jnp.exp2(scores - highest)
    keep = jnp.exp2(before - highest)
    top[...] = jnp.broadcast_to(highest, top.shape)
    total[...] = total[...] * keep + jnp.sum(weights, axis=1, keepdims=True)
    acc[...] = acc[...] * keep + jnp.dot(
        weights.astype(jnp.bfloat16), v_ref[...], preferred_element_type=jnp.float32
    )

    @pl.when(p == pl.num_programs(0) - 1)
    def _():
        result = acc[...] / total[:, :1]
        per_group = heads // G
        per_chunk = per_group // chunks
        for c in range(chunks):
            for g in range(G):
                for h in range(per_chunk):
                    begin = (c * G + g) * PACK + h * steps
                    head = g * per_group + c * per_chunk + h
                    out_ref[:, head * HD : (head + 1) * HD] = result[
                        begin : begin + steps
                    ].astype(jnp.bfloat16)


def attend(packed, cache_keys, cache_values, lengths, heads, steps, keyval_real):
    chunks, G = packed.shape[0] - 1, packed.shape[1]
    query_rows = chunks * G * PACK
    cache_len = cache_keys.shape[0]
    span = 1024
    whole = pl.BlockSpec(packed.shape, lambda p: (0, 0, 0, 0))
    return pl.pallas_call(
        functools.partial(attend_kernel, (heads, steps, keyval_real)),
        grid=(cache_len // span,),
        out_shape=(
            jax.ShapeDtypeStruct((steps, heads * HD), jnp.bfloat16),
            jax.ShapeDtypeStruct((steps, 2 * HD), jnp.bfloat16),
        ),
        in_specs=[
            pl.BlockSpec(memory_space=pltpu.SMEM),
            whole,
            pl.BlockSpec((span, HD), lambda p: (p, 0)),
            pl.BlockSpec((span, HD), lambda p: (p, 0)),
        ],
        out_specs=(
            pl.BlockSpec((steps, heads * HD), lambda p: (0, 0)),
            pl.BlockSpec((steps, 2 * HD), lambda p: (0, 0)),
        ),
        scratch_shapes=[
            pltpu.VMEM((query_rows, HD), jnp.float32),
            pltpu.VMEM((query_rows, LANES), jnp.float32),
            pltpu.VMEM((query_rows, LANES), jnp.float32),
        ],
        compiler_params=pltpu.CompilerParams(vmem_limit_bytes=32 * 2**20),
        cost_estimate=pl.CostEstimate(
            flops=4 * query_rows * cache_len * HD,
            bytes_accessed=4 * cache_len * HD,
            transcendentals=query_rows * cache_len,
        ),
    )(lengths, packed, cache_keys, cache_values)


def on_device(tokens, norm_gain, w_query, w_keyval, cache_keys, cache_values, lengths):
    inputs = tokens[0]
    steps = inputs.shape[1]
    Y, Z = lax.axis_size("gy"), lax.axis_size("gz")
    heads = w_query.shape[1] * Y // HD
    keyval_real = w_keyval.shape[1] // Z
    missing = -keyval_real % LANES
    if missing:
        split = w_keyval.reshape(w_keyval.shape[0], Z, keyval_real)
        w_keyval = jnp.pad(split, ((0, 0), (0, 0), (0, missing))).reshape(w_keyval.shape[0], -1)
    packed = project(inputs, norm_gain, w_query, w_keyval)
    attended, entries = attend(
        packed, cache_keys[0, 0], cache_values[0, 0], lengths, heads, steps, keyval_real
    )
    return (attended[None, None], entries[None, None])


def solution(mesh):
    return jax.shard_map(
        on_device,
        mesh=mesh,
        in_specs=(
            P("gz", "gy", None, "gx"),
            P("gx"),
            P("gx", "gy"),
            P("gx", "gy"),
            P("gz", ("gx", "gy"), None, None),
            P("gz", ("gx", "gy"), None, None),
            P("gz", ("gx", "gy")),
        ),
        out_specs=(P("gz", ("gx", "gy"), None, None), P("gz", ("gx", "gy"), None, None)),
        check_vma=False,
    )
```

time: 237 us -> 53.4 us (0.23)
  blocking collectives: 120 us -> 0 us
  matrix products: 50.2 us -> 0 us
  Pallas kernels: 0 us -> 45.8 us
  starting transfers between devices: 25.9 us -> 0 us
  waiting for transfers between devices: 19.3 us -> 0 us
  other arithmetic: 8.9 us -> 0 us
  local copies, waits for them, and re-layouts: 9.57 us -> 6 us
    unnamed x1 -> x0, blocking collectives: 78.4 us -> none
    dot_general x12 -> x0, matrix products: 50.2 us -> none  [the longest x4 44 us: project(): jnp.dot(row_block, w_query, preferred_element_type=jnp.float32)]
    pallas_call x0 -> x2, Pallas kernels: none -> 45.8 us  [the longest x1 37.5 us: project(): pl.pallas_call(functools.partial(project_kernel, (X, Y, Z, seqs, steps)),...]
    all_to_all x8 -> x0, starting transfers between devices: 25.9 us -> none  [the longest x4 13.2 us: project(): lax.all_to_all(summed[:, :, :query_width], 'gy', split_axis=0, concat_axi...]
    psum x1 -> x0, blocking collectives: 23.1 us -> none  [normalize(): lax.psum((jnp.sum(values, axis=-1), jnp.sum(values * values, axis=-1)), '...]
    all_to_all x8 -> x0, waiting for transfers between devices: 19.3 us -> none  [the longest x4 10.6 us: project(): lax.all_to_all(summed[:, :, :query_width], 'gy', split_axis=0, concat_axi...]
    all_gather x4 -> x0, blocking collectives: 18.6 us -> none  [project(): gathered = lax.all_gather(normed, 'gy', axis=0, tiled=True)]
    slice x8 -> x0, other arithmetic: 5.29 us -> none  [the longest x4 2.71 us: project(): summed[:, :, :query_width]]
  transfers between devices with their start and end apart: 8 -> 0, of which waited for: 8 -> 0; matrix products, arithmetic and copies ran while one was open for 4% -> 0% of each run, Pallas kernels for 0% -> 0%
where the time goes in v1:
time: 53.4 us; the launch traced here: 53.1 us
  Pallas kernels  45.8 us (86%)
  local copies, waits for them, and re-layouts  6 us (11%)
  between operations  1.3 us (2%)
    pallas_call x1, Pallas kernels, project(): pl.pallas_call(functools.partial(project_kernel, (X, Y, Z, seqs, steps)),...  37.5 us
    pallas_call x1, Pallas kernels, attend(): pl.pallas_call(functools.partial(attend_kernel, (heads, steps, keyval_rea...  8.31 us
    unnamed x6, local copies, waits for them, and re-layouts  3.09 us
    another operation x1, local copies, waits for them, and re-layouts, project(): tokens.reshape(block, depth)  1.6 us
    reshape x1, local copies, waits for them, and re-layouts, project(): gain.reshape(1, depth)  1.31 us

profile of v1, /device:TPU:0, one launch (start us, length us, event | category | flops | bytes accessed | tf_op | source)
XLA Modules:
  0.0 53.1 jit_solution(15423997727263133080)
XLA Ops:
  0.6 1.6 %reshape_squeeze.3.x_ref = bf16[32,2304]{1,0:T(8,128)(2,1)} reshape(bf16[1,8,4,2304]{3,2,1,0:T(4,128)(2,1)} %param.7) | data formatting | bytes 294912 | tf_op jit(solution)/shard_map/reshape;squeeze | solution.py:365
  2.2 1.3 %reshape.7.gain_ref = f32[1,2304]{1,0:T(1,128)} reshape(f32[2304]{0:T(1024)} %param.8) | data formatting | bytes 18432 | tf_op jit(solution)/shard_map/reshape | solution.py:365
  3.5 0.0 copy-start
  3.5 37.5 %shard_map.86.q_ref = bf16[4,4,16,256]{3,2,1,0:T(8,128)(2,1)} custom-call(bf16[32,2304]{1,0:T(8,128)(2,1)} %reshape_squeeze.3.x_ref, f32[1,2304]{1,0:T(1,128)} %reshape.7.gain_ref, bf16[2304,6144]{1,0:T(8,128)(2,1)} %wq_hbm.1, bf16[2304,256]{1,0:T(8,128)(2,1)} %wkv_hbm.1), custom_call_target="tpu_custom_call" | custom-call | flops 1887436800 | bytes 14745600 | tf_op jit(solution)/shard_map/pallas_call | solution.py:323
  41.7 0.0 copy-done
  41.7 0.0 copy-start.1
  41.8 2.2 %copy-done.1 = bf16[1,1,8192,256]{3,2,1,0:T(8,128)(2,1)S(1)} copy-done((bf16[1,1,8192,256]{3,2,1,0:T(8,128)(2,1)S(1)}, bf16[1,1,8192,256]{3,2,1,0:T(8,128)(2,1)}, u32[]{:S(2)}) %copy-start.1) | copy-done | bytes 4194328
  43.9 0.0 copy-start.2
  43.9 0.9 %copy-done.2 = bf16[4,4,16,256]{3,2,1,0:T(8,128)(2,1)S(1)} copy-done((bf16[4,4,16,256]{3,2,1,0:T(8,128)(2,1)S(1)}, bf16[4,4,16,256]{3,2,1,0:T(8,128)(2,1)}, u32[]{:S(2)}) %copy-start.2) | copy-done | bytes 131096
  44.8 8.3 %shard_map.87 = (bf16[4,12288]{1,0:T(4,128)(2,1)}, bf16[4,512]{1,0:T(4,128)(2,1)}) custom-call(s32[1,1]{1,0:T(1,128)S(6)} %copy.9.len_ref, bf16[4,4,16,256]{3,2,1,0:T(8,128)(2,1)S(1)} %copy-done.2, bf16[8192,256]{1,0:T(8,128)(2,1)S(1)} %bitcast.4, bf16[8192,256]{1,0:T(8,128)(2,1)S(1)} %bitcast.5), custom_call_target="tpu_custom_call" | custom-call | flops 1610612736 | bytes 8388608 | tf_op jit(solution)/shard_map/pallas_call | solution.py:434
Async XLA Ops:
  3.5 38.2 %copy-start = (bf16[1,1,8192,256]{3,2,1,0:T(8,128)(2,1)S(1)}, bf16[1,1,8192,256]{3,2,1,0:T(8,128)(2,1)}, u32[]{:S(2)}) copy-start(bf16[1,1,8192,256]{3,2,1,0:T(8,128)(2,1)} %param.11) | copy-start | bytes 12582916
  41.7 2.2 %copy-start.1 = (bf16[1,1,8192,256]{3,2,1,0:T(8,128)(2,1)S(1)}, bf16[1,1,8192,256]{3,2,1,0:T(8,128)(2,1)}, u32[]{:S(2)}) copy-start(bf16[1,1,8192,256]{3,2,1,0:T(8,128)(2,1)} %param.12) | copy-start | bytes 12582916
  43.9 0.9 %copy-start.2 = (bf16[4,4,16,256]{3,2,1,0:T(8,128)(2,1)S(1)}, bf16[4,4,16,256]{3,2,1,0:T(8,128)(2,1)}, u32[]{:S(2)}) copy-start(bf16[4,4,16,256]{3,2,1,0:T(8,128)(2,1)} %shard_map.86.q_ref) | copy-start | bytes 393220

commit v2 on v1

--- a/solution.py
+++ b/solution.py
@@ -13,6 +13,8 @@
 OUTER = 4
 LANES = 128
 PACK = 16
+AHEAD = 2
+WIDTH = 512
 MESH = pl.DeviceIdType.MESH
 
 
@@ -25,9 +27,12 @@
     out_ref,
     wq,
     wkv,
+    raw,
     rows,
     stat_send,
     stat_recv,
+    scale_send,
+    scale_recv,
     product,
     a_send,
     a_recv,
@@ -40,6 +45,8 @@
     w_sem,
     st_ssem,
     st_rsem,
+    sc_ssem,
+    sc_rsem,
     y_ssem,
     y_rsem,
     k_ssem,
@@ -64,6 +71,8 @@
     width = a_send.shape[-1]
     query_chunks = query_half // width
     chunks = query_chunks + 1
+    packs = c_send.shape[0]
+    subs = query_chunks // (packs - 1)
 
     i = lax.axis_index("gx")
     j = lax.axis_index("gy")
@@ -107,7 +116,15 @@
                     device_id_type=MESH,
                 )
 
-    values = x_ref[...].astype(jnp.float32)
+    values = jnp.concatenate(
+        [x_ref[0, q].astype(jnp.float32) for q in range(seqs)], axis=0
+    )
+
+    def row_range(dj, dk):
+        g = ((j + Y - dj) % Y) * Z + (k + Z - dk) % Z
+        return pl.ds(pl.multiple_of(g * block, block), block)
+
+    raw[row_range(0, 0), :] = values.astype(jnp.bfloat16)
     row_sum = jnp.sum(values, axis=1, keepdims=True)
     row_square = jnp.sum(values * values, axis=1, keepdims=True)
     lane = lax.broadcasted_iota(jnp.int32, (block, LANES), 1)
@@ -138,44 +155,73 @@
         send(stat_send, stat_recv.at[d], st_ssem.at[d], st_rsem.at[d], (i + d) % X, j, k)
         for d in range(1, X)
     ]
+
+    def raw_block(dj):
+        return raw.at[row_range(dj, 0), :]
+
+    y_copies = [None] + [
+        send(raw_block(0), raw_block(0), y_ssem.at[dj], y_rsem.at[dj], i, (j + dj) % Y, k)
+        for dj in range(1, Y)
+    ]
+    k_copies = {}
+
+    def pass_on(dj):
+        for dk in range(1, Z):
+            k_copies[dj, dk] = send(
+                raw_block(dj),
+                raw_block(dj),
+                k_ssem.at[dj, dk],
+                k_rsem.at[dj, dk],
+                i,
+                j,
+                (k + dk) % Z,
+            )
+
+    pass_on(0)
     total = stat_send[...]
     for d in range(1, X):
         stat_copies[d - 1].wait_recv()
         total = total + stat_recv[d]
-    total = jnp.concatenate((total, jnp.zeros((LANES - 8, LANES), jnp.float32)), axis=0).T
-    center = total[:block, 0:1] / D
-    spread = total[:block, 1:2] / D - center * center
-    factor = lax.rsqrt(spread + 1e-05)
-    normed = ((x_ref[...].astype(jnp.float32) - center) * factor * gain_ref[...]).astype(jnp.bfloat16)
-    own_rows = pl.ds(pl.multiple_of(me * block, block), block)
-    rows[own_rows, :] = normed
-
-    def row_block(dj):
-        g = ((j + Y - dj) % Y) * Z + k
-        return rows.at[pl.ds(pl.multiple_of(g * block, block), block), :]
-
-    y_copies = [None] + [
-        send(row_block(0), row_block(0), y_ssem.at[dj], y_rsem.at[dj], i, (j + dj) % Y, k)
-        for dj in range(1, Y)
-    ]
-    k_copies = []
+    center = total[0:1] / D
+    spread = total[1:2] / D - center * center
+    scale_send[...] = jnp.concatenate(
+        (center, lax.rsqrt(spread + 1e-05), jnp.zeros((6, LANES), jnp.float32)), axis=0
+    )
+    scale_copies = {}
     for dj in range(Y):
-        if dj:
-            y_copies[dj].wait_recv()
-        for dk in range(1, Z):
-            k_copies.append(
-                send(
-                    row_block(dj),
-                    row_block(dj),
-                    k_ssem.at[dj, dk],
-                    k_rsem.at[dj, dk],
+        for dk in range(Z):
+            if dj or dk:
+                slot = dj * Z + dk
+                scale_copies[slot] = send(
+                    scale_send,
+                    scale_recv.at[slot],
+                    sc_ssem.at[slot],
+                    sc_rsem.at[slot],
                     i,
-                    j,
+                    (j + dj) % Y,
                     (k + dk) % Z,
                 )
-            )
-    for copy in k_copies:
+    for dj in range(1, Y):
+        y_copies[dj].wait_recv()
+        pass_on(dj)
+    for copy in scale_copies.values():
         copy.wait_recv()
+    scales = [scale_send[...]] + [scale_recv[slot] for slot in range(1, G)]
+    if 8 * G < LANES:
+        scales.append(jnp.zeros((LANES - 8 * G, LANES), jnp.float32))
+    scales = jnp.concatenate(scales, axis=0).T
+    gain = gain_ref[...].reshape(1, gain_ref.shape[0])
+    for dk in range(Z):
+        for dj in range(Y):
+            if dk:
+                k_copies[dj, dk].wait_recv()
+            here = row_range(dj, dk)
+            slot = dj * Z + dk
+            center = scales[:block, 8 * slot : 8 * slot + 1]
+            factor = scales[:block, 8 * slot + 1 : 8 * slot + 2]
+            rows[here, :] = (
+                (raw[here, :].astype(jnp.float32) - center) * factor * gain
+            ).astype(jnp.bfloat16)
 
     def multiply(c):
         loads[c].wait()
@@ -254,11 +300,17 @@
         own[c, :, :w] = kept[c, zi, :, :w]
 
     def stage_c(c):
-        w = chunk_width(c)
-        part = own[c, :, :w]
-        for dz in range(1, NZ):
-            b_copies[c, dz].wait_recv()
-            part = part + b_recv[c, dz, :, :w].astype(jnp.float32)
+        members = range(c * subs, (c + 1) * subs) if c < packs - 1 else [query_chunks]
+        parts = []
+        for m in members:
+            w = chunk_width(m)
+            part = own[m, :, :w]
+            for dz in range(1, NZ):
+                b_copies[m, dz].wait_recv()
+                part = part + b_recv[m, dz, :, :w].astype(jnp.float32)
+            parts.append(part)
+        part = jnp.concatenate(parts, axis=1)
+        w = part.shape[1]
         for dj in range(Y):
             for dk in range(Z):
                 begin = (dk * Y + dj) * steps
@@ -289,14 +341,18 @@
                     )
         c_recv[c, me] = c_send[c, me]
 
-    for c in range(chunks + 2):
+    done = 0
+    for c in range(chunks + AHEAD):
         if c < chunks:
             multiply(c)
             stage_a(c)
-        if 1 <= c < chunks + 1:
-            stage_b(c - 1)
-        if 2 <= c:
-            stage_c(c - 2)
+        if c >= AHEAD:
+            stage_b(c - AHEAD)
+            if done < packs - 1 and c - AHEAD >= (done + 1) * subs + 1:
+                stage_c(done)
+                done += 1
+    for c in range(done, packs):
+        stage_c(c)
     for copy in c_copies.values():
         copy.wait_recv()
     out_ref[...] = c_recv[...]
@@ -306,7 +362,7 @@
 
 def project(tokens, gain, w_query, w_keyval):
     X, Y, Z = lax.axis_size("gx"), lax.axis_size("gy"), lax.axis_size("gz")
-    seqs, steps, depth = tokens.shape
+    seqs, steps, depth = tokens.shape[1:]
     G = Y * Z
     NZ = OUTER
     NX = X // NZ
@@ -314,23 +370,28 @@
     dest_rows = Z * Y * steps
     query_half = w_query.shape[1] // Z
     keyval_half = w_keyval.shape[1] // Z
-    width = min(query_half, HD * (PACK // steps))
+    pack_width = min(query_half, HD * (PACK // steps))
+    width = WIDTH if pack_width % WIDTH == 0 else pack_width
     chunks = query_half // width + 1
+    packs = query_half // pack_width + 1
     bf16, f32 = jnp.bfloat16, jnp.float32
     any_space = pl.BlockSpec(memory_space=pl.ANY)
     vmem = pl.BlockSpec(memory_space=pltpu.VMEM)
     dma = pltpu.SemaphoreType.DMA
     return pl.pallas_call(
         functools.partial(project_kernel, (X, Y, Z, seqs, steps)),
-        out_shape=jax.ShapeDtypeStruct((chunks, G, PACK, HD), bf16),
+        out_shape=jax.ShapeDtypeStruct((packs, G, PACK, HD), bf16),
         in_specs=[vmem, vmem, any_space, any_space],
         out_specs=vmem,
         scratch_shapes=[
             pltpu.VMEM((depth, query_half), bf16),
             pltpu.VMEM((depth, keyval_half), bf16),
             pltpu.VMEM((G * block, depth), bf16),
+            pltpu.VMEM((G * block, depth), bf16),
             pltpu.VMEM((8, LANES), f32),
             pltpu.VMEM((X, 8, LANES), f32),
+            pltpu.VMEM((8, LANES), f32),
+            pltpu.VMEM((G, 8, LANES), f32),
             pltpu.VMEM((G * block, width), f32),
             pltpu.VMEM((chunks, NX, NZ * dest_rows, width), bf16),
             pltpu.VMEM((chunks, NX, NZ * dest_rows, width), bf16),
@@ -338,11 +399,13 @@
             pltpu.VMEM((chunks, NZ, dest_rows, width), bf16),
             pltpu.VMEM((chunks, NZ, dest_rows, width), bf16),
             pltpu.VMEM((chunks, dest_rows, width), f32),
-            pltpu.VMEM((chunks, G, PACK, HD), bf16),
-            pltpu.VMEM((chunks, G, PACK, HD), bf16),
+            pltpu.VMEM((packs, G, PACK, HD), bf16),
+            pltpu.VMEM((packs, G, PACK, HD), bf16),
             dma((chunks,)),
             dma((X,)),
             dma((X,)),
+            dma((G,)),
+            dma((G,)),
             dma((Y,)),
             dma((Y,)),
             dma((Y, Z)),
@@ -351,18 +414,18 @@
             dma((chunks, NX)),
             dma((chunks, NZ)),
             dma((chunks, NZ)),
-            dma((chunks, G)),
-            dma((chunks, G)),
+            dma((packs, G)),
+            dma((packs, G)),
         ],
         compiler_params=pltpu.CompilerParams(
-            collective_id=0, has_side_effects=True, vmem_limit_bytes=56 * 2**20
+            collective_id=0, has_side_effects=True, vmem_limit_bytes=32 * 2**20
         ),
         cost_estimate=pl.CostEstimate(
             flops=2 * G * block * depth * (query_half + keyval_half),
             bytes_accessed=2 * depth * (query_half + keyval_half),
             transcendentals=0,
         ),
-    )(tokens.reshape(block, depth), gain.reshape(1, depth), w_query, w_keyval)
+    )(tokens, gain, w_query, w_keyval)
 
 
 def attend_kernel(sizes, len_ref, q_ref, k_ref, v_ref, out_ref, new_ref, acc, top, total):
@@ -429,7 +492,7 @@
     chunks, G = packed.shape[0] - 1, packed.shape[1]
     query_rows = chunks * G * PACK
     cache_len = cache_keys.shape[0]
-    span = 1024
+    span = 2048
     whole = pl.BlockSpec(packed.shape, lambda p: (0, 0, 0, 0))
     return pl.pallas_call(
         functools.partial(attend_kernel, (heads, steps, keyval_real)),
@@ -463,8 +526,7 @@
 
 
 def on_device(tokens, norm_gain, w_query, w_keyval, cache_keys, cache_values, lengths):
-    inputs = tokens[0]
-    steps = inputs.shape[1]
+    steps = tokens.shape[2]
     Y, Z = lax.axis_size("gy"), lax.axis_size("gz")
     heads = w_query.shape[1] * Y // HD
     keyval_real = w_keyval.shape[1] // Z
@@ -472,7 +534,7 @@
     if missing:
         split = w_keyval.reshape(w_keyval.shape[0], Z, keyval_real)
         w_keyval = jnp.pad(split, ((0, 0), (0, 0), (0, missing))).reshape(w_keyval.shape[0], -1)
-    packed = project(inputs, norm_gain, w_query, w_keyval)
+    packed = project(tokens, norm_gain, w_query, w_keyval)
     attended, entries = attend(
         packed, cache_keys[0, 0], cache_values[0, 0], lengths, heads, steps, keyval_real
     )

time: 53.4 us -> 45.2 us (0.85)
  Pallas kernels: 45.8 us -> 40.7 us
  local copies, waits for them, and re-layouts: 6 us -> 2.89 us
    pallas_call x1, Pallas kernels: 37.5 us -> 33.4 us  [project(): pl.pallas_call(functools.partial(project_kernel, (X, Y, Z, seqs, steps)),...]
    another operation x1 -> x0, local copies, waits for them, and re-layouts: 1.6 us -> none  [project(): tokens.reshape(block, depth)]
    reshape x1 -> x0, local copies, waits for them, and re-layouts: 1.31 us -> none  [project(): gain.reshape(1, depth)]
    pallas_call x1, Pallas kernels: 8.31 us -> 7.31 us  [attend(): pl.pallas_call(functools.partial(attend_kernel, (heads, steps, keyval_rea...]
    unnamed x6 -> x10, local copies, waits for them, and re-layouts: 3.09 us -> 2.89 us
where the time goes in v2:
time: 45.2 us; the launch traced here: 44.9 us
  Pallas kernels  40.7 us (90%)
  local copies, waits for them, and re-layouts  2.89 us (6%)
  between operations  1.31 us (3%)
    pallas_call x1, Pallas kernels, project(): pl.pallas_call(functools.partial(project_kernel, (X, Y, Z, seqs, steps)),...  33.4 us
    pallas_call x1, Pallas kernels, attend(): pl.pallas_call(functools.partial(attend_kernel, (heads, steps, keyval_rea...  7.31 us
    unnamed x10, local copies, waits for them, and re-layouts  2.89 us

profile of v2, /device:TPU:0, one launch (start us, length us, event | category | flops | bytes accessed | tf_op | source)
XLA Modules:
  0.0 44.9 jit_solution(8765574891583893354)
XLA Ops:
  1.3 0.0 copy-start.2
  1.3 1.3 %copy-done.2 = bf16[2304,256]{1,0:T(8,128)(2,1)S(1)} copy-done((bf16[2304,256]{1,0:T(8,128)(2,1)S(1)}, bf16[2304,256]{1,0:T(8,128)(2,1)}, u32[]{:S(2)}) %copy-start.2) | copy-done | bytes 1179672
  2.6 0.0 copy-start.3
  2.6 0.9 %copy-done.3 = bf16[1,8,4,2304]{3,2,1,0:T(4,128)(2,1)S(1)} copy-done((bf16[1,8,4,2304]{3,2,1,0:T(4,128)(2,1)S(1)}, bf16[1,8,4,2304]{3,2,1,0:T(4,128)(2,1)}, u32[]{:S(2)}) %copy-start.3) | copy-done | bytes 147480
  3.5 0.0 copy-start.4
  3.5 0.7 %copy-done.4 = f32[2304]{0:T(1024)S(1)} copy-done((f32[2304]{0:T(1024)S(1)}, f32[2304]{0:T(1024)}, u32[]{:S(2)}) %copy-start.4) | copy-done | bytes 9240
  4.2 0.0 copy-start
  4.2 0.0 copy-start.1
  4.2 33.4 %shard_map.86.q_ref = bf16[4,4,16,256]{3,2,1,0:T(8,128)(2,1)S(1)} custom-call(bf16[1,8,4,2304]{3,2,1,0:T(4,128)(2,1)S(1)} %copy-done.3, f32[2304]{0:T(1024)S(1)} %copy-done.4, bf16[2304,6144]{1,0:T(8,128)(2,1)} %wq_hbm.1, bf16[2304,256]{1,0:T(8,128)(2,1)S(1)} %copy-done.2), custom_call_target="tpu_custom_call" | custom-call | flops 1887436800 | bytes 14745600 | tf_op jit(solution)/shard_map/pallas_call | solution.py:381
  37.6 0.0 copy-done
  37.6 0.0 copy-done.1
  37.6 7.3 %shard_map.87 = (bf16[4,12288]{1,0:T(4,128)(2,1)}, bf16[4,512]{1,0:T(4,128)(2,1)}) custom-call(s32[1,1]{1,0:T(1,128)S(6)} %copy.9.len_ref, bf16[4,4,16,256]{3,2,1,0:T(8,128)(2,1)S(1)} %shard_map.86.q_ref, bf16[8192,256]{1,0:T(8,128)(2,1)S(1)} %bitcast.4, bf16[8192,256]{1,0:T(8,128)(2,1)S(1)} %bitcast.5), custom_call_target="tpu_custom_call" | custom-call | flops 1610612736 | bytes 8388608 | tf_op jit(solution)/shard_map/pallas_call | solution.py:497
Async XLA Ops:
  1.3 1.3 %copy-start.2 = (bf16[2304,256]{1,0:T(8,128)(2,1)S(1)}, bf16[2304,256]{1,0:T(8,128)(2,1)}, u32[]{:S(2)}) copy-start(bf16[2304,256]{1,0:T(8,128)(2,1)} %wkv_hbm.1) | copy-start | bytes 3538948
  2.6 0.9 %copy-start.3 = (bf16[1,8,4,2304]{3,2,1,0:T(4,128)(2,1)S(1)}, bf16[1,8,4,2304]{3,2,1,0:T(4,128)(2,1)}, u32[]{:S(2)}) copy-start(bf16[1,8,4,2304]{3,2,1,0:T(4,128)(2,1)} %x_ref.1) | copy-start | bytes 442372
  3.5 0.7 %copy-start.4 = (f32[2304]{0:T(1024)S(1)}, f32[2304]{0:T(1024)}, u32[]{:S(2)}) copy-start(f32[2304]{0:T(1024)} %gain_ref.1) | copy-start | bytes 27652
  4.2 33.5 %copy-start = (bf16[1,1,8192,256]{3,2,1,0:T(8,128)(2,1)S(1)}, bf16[1,1,8192,256]{3,2,1,0:T(8,128)(2,1)}, u32[]{:S(2)}) copy-start(bf16[1,1,8192,256]{3,2,1,0:T(8,128)(2,1)} %param.11) | copy-start | bytes 12582916
  4.2 33.5 %copy-start.1 = (bf16[1,1,8192,256]{3,2,1,0:T(8,128)(2,1)S(1)}, bf16[1,1,8192,256]{3,2,1,0:T(8,128)(2,1)}, u32[]{:S(2)}) copy-start(bf16[1,1,8192,256]{3,2,1,0:T(8,128)(2,1)} %param.12) | copy-start | bytes 12582916
